TPU v7x, 512 devices: a whole 4x4x16 slice. The times are simulated.
512 devices in a mesh: src: 32 (over z, core), tgt: 16 (over y, x).
Axes of the slice: x: 4, y: 4, z: 16, core: 2. Of those that a mesh axis runs over, the one named last changes fastest.
Arguments:
- source_cells: bfloat16 [32768, 512], P('src'), may hold values from -6 to 6
- target_cells: bfloat16 [16384, 512], P('tgt'), may hold values from -6 to 6
- source_mass: float32 [32768], P('src'), may hold values from 0.25 to 4
- target_mass: float32 [16384], P('tgt'), may hold values from 0.25 to 4
- source_order: int32 [32768], P('src'), may hold values from 0 to 1023, as said below
- tile_list: int32 [32, 192], P('src', 'tgt'), may hold values from -1 to 15, as said below
- tile_count: int32 [32, 16], P('src', 'tgt'), may hold values from 4 to 12, as said below
Outputs:
- projected: bfloat16 [32768, 512], P(('src', 'tgt'))
- log_mass: float32 [32768], P(('src', 'tgt'))
Inputs may be any that keep to these rules, and one draw needn't show every extreme that they name: `source_order`: each block of 1024 entries is a permutation of 0 to 1023. `tile_list`: the live entries of one list are distinct codes p * 4 + q of local block pairs, and every local source block and every local target block of the pair of shards occurs among them; entries past the count are -1. `tile_count`: counts vary from pair to pair of shards; some pair has 12.
All inputs are finite; a program needn't handle non-finite values.
Results may differ from a plain program's by a relative error of at most 0.009.
Values sent between devices are 32-bit elements; how exact they have to be, the bound alone decides.
A program may use at most 64 MiB of HBM per device.

v0:
```python
import jax
import jax.numpy as jnp
from jax import lax
from jax.sharding import PartitionSpec as P

EMB = 512
BLK = 256
ITERS = 3


INVERSE_TEMP = 64.0
MASS_POWER = 0.8
NORM_EPSILON = 1e-06


def normalized(embedded):
    widened = embedded.astype(jnp.float32)
    scaled = widened * lax.rsqrt(jnp.mean(widened * widened, axis=1, keepdims=True) + NORM_EPSILON)
    return scaled.astype(jnp.bfloat16)


def body(source_cells, target_cells, source_mass, target_mass, source_order, tile_list, tile_count):
    src_count = source_cells.shape[0]
    tgt_count = target_cells.shape[0]
    tgt_blocks = tgt_count // BLK
    src_hat = normalized(source_cells[source_order])
    sorted_mass = source_mass[source_order]
    tgt_hat = normalized(target_cells)
    tile_codes = tile_list.reshape(-1)
    tile_total = tile_count.reshape(())
    sharpness = INVERSE_TEMP / EMB

    def make_tile(tile_slot):
        code_now = tile_codes[tile_slot]
        src_block = code_now // tgt_blocks
        tgt_block = code_now % tgt_blocks
        src_rows = lax.dynamic_slice_in_dim(src_hat, src_block * BLK, BLK, 0)
        tgt_rows = lax.dynamic_slice_in_dim(tgt_hat, tgt_block * BLK, BLK, 0)
        similarity = lax.dot_general(
            src_rows, tgt_rows, (((1,), (1,)), ((), ())), preferred_element_type=jnp.float32
        )
        return (src_block, tgt_block, jnp.exp(similarity * sharpness))

    tgt_scale = jnp.ones((tgt_count,), jnp.float32)
    src_scale = jnp.ones((src_count,), jnp.float32)
    for rounds in range(ITERS):
        row_weights = tgt_scale

        def row_add_tile(tile_slot, running):
            src_block, tgt_block, kernel = make_tile(tile_slot)
            contrib = jnp.dot(
                kernel,
                lax.dynamic_slice_in_dim(row_weights, tgt_block * BLK, BLK, 0),
                precision=lax.Precision.HIGHEST,
            )
            current = lax.dynamic_slice_in_dim(running, src_block * BLK, BLK, 0)
            return lax.dynamic_update_slice_in_dim(running, current + contrib, src_block * BLK, 0)

        row_total = lax.psum(
            lax.fori_loop(0, tile_total, row_add_tile, jnp.zeros((src_count,), jnp.float32)), "tgt"
        )
        src_scale = (sorted_mass / row_total) ** MASS_POWER
        weights = src_scale

        def col_add_tile(tile_slot, running):
            src_block, tgt_block, kernel = make_tile(tile_slot)
            contrib = jnp.dot(
                lax.dynamic_slice_in_dim(weights, src_block * BLK, BLK, 0),
                kernel,
                precision=lax.Precision.HIGHEST,
            )
            current = lax.dynamic_slice_in_dim(running, tgt_block * BLK, BLK, 0)
            return lax.dynamic_update_slice_in_dim(running, current + contrib, tgt_block * BLK, 0)

        col_total = lax.psum(
            lax.fori_loop(0, tile_total, col_add_tile, jnp.zeros((tgt_count,), jnp.float32)), "src"
        )
        tgt_scale = (target_mass / col_total) ** MASS_POWER

    def add_projection(tile_slot, carried):
        numerator, row_mass = carried
        src_block, tgt_block, kernel = make_tile(tile_slot)
        weighted = kernel * lax.dynamic_slice_in_dim(tgt_scale, tgt_block * BLK, BLK, 0)[None, :]
        tgt_rows = lax.dynamic_slice_in_dim(target_cells, tgt_block * BLK, BLK, 0)
        contrib = jnp.dot(
            weighted.astype(jnp.bfloat16), tgt_rows, preferred_element_type=jnp.float32
        )
        current = lax.dynamic_slice_in_dim(numerator, src_block * BLK, BLK, 0)
        numerator = lax.dynamic_update_slice_in_dim(
            numerator, current + contrib, src_block * BLK, 0
        )
        mass_now = lax.dynamic_slice_in_dim(row_mass, src_block * BLK, BLK, 0)
        row_mass = lax.dynamic_update_slice_in_dim(
            row_mass, mass_now + jnp.sum(weighted, axis=1), src_block * BLK, 0
        )
        return (numerator, row_mass)

    empty = (jnp.zeros((src_count, EMB), jnp.float32), jnp.zeros((src_count,), jnp.float32))
    numerator, row_mass = lax.fori_loop(0, tile_total, add_projection, empty)
    numerator = jnp.zeros_like(numerator).at[source_order].set(numerator)
    row_mass = jnp.zeros_like(row_mass).at[source_order].set(row_mass)
    src_scale = jnp.zeros_like(src_scale).at[source_order].set(src_scale)
    my_rows = src_count // lax.axis_size("tgt")
    my_start = lax.axis_index("tgt") * my_rows
    my_numerator, my_mass = (
        lax.psum_scatter(numerator, "tgt", scatter_dimension=0, tiled=True),
        lax.psum_scatter(row_mass, "tgt", scatter_dimension=0, tiled=True),
    )
    my_scale = lax.dynamic_slice_in_dim(src_scale, my_start, my_rows, 0)
    projected = (my_numerator / my_mass[:, None]).astype(jnp.bfloat16)
    log_mass = jnp.log(my_scale) + jnp.log(my_mass)
    return (projected, log_mass)


def solution(mesh):
    placed = (
        P("src", None),
        P("tgt", None),
        P("src"),
        P("tgt"),
        P("src"),
        P("src", "tgt"),
        P("src", "tgt"),
    )
    return jax.shard_map(
        body,
        mesh=mesh,
        in_specs=placed,
        out_specs=(P(("src", "tgt"), None), P(("src", "tgt"))),
        check_vma=False,
    )
```

profile of v0, /device:TPU:1, one launch (start us, length us, event | category | flops | bytes accessed | tf_op | source)
XLA Modules:
  0.0 779.5 jit_solution(9880189005637239479)
XLA Ops:
  8.4 5.1 gather_fusion
  15.3 4.5 gather_fusion.1
  21.9 39.8 %while.86 = (s32[]{:T(128)}, f32[1024]{0:T(1024)S(1)}, s32[]{:T(128)}, s32[12]{0:T(128)S(1)}, bf16[1024,512]{1,0:T(8,128)(2,1)S(1)}, /*index=5*/bf16[1024,512]{1...) while((s32[]{:T(128)}, f32[1024]{0:T(1024)S(1)}, ...), condition=%wide.region_3.4_spmd, body=%wide.region_2.3_spmd.sunk | while | flops 67961120 | bytes 1053158 | solution.py:60
  61.7 40.7 %psum.42 = f32[1024]{0:T(1024)S(1)} all-reduce(f32[1024]{0:T(1024)S(1)} %get-tuple-element.680), channel_id=1, replica_groups=mesh['src'=32,'tgt'=16] {'tgt'}, use_global_device_ids=true, to_apply=%region_4.5 | all-reduce | flops 1024 | bytes 8192 | tf_op jit(solution)/shard_map/psum | solution.py:59
  102.5 39.6 %while.87 = (s32[]{:T(128)}, f32[1024]{0:T(1024)S(1)}, s32[]{:T(128)}, s32[12]{0:T(128)S(1)}, f32[1024]{0:T(1024)S(1)}, /*index=5*/bf16[1024,512]{1,0:T(8,128)(2...) while((s32[]{:T(128)}, f32[1024]{0:T(1024)S(1)}, ...), condition=%wide.region_6.7_spmd, body=%wide.region_5.6_spmd.sunk | while | flops 67961120 | bytes 1056242 | solution.py:76
  142.1 72.5 %psum.43 = f32[1024]{0:T(1024)S(1)} all-reduce(f32[1024]{0:T(1024)S(1)} %get-tuple-element.681), channel_id=1, replica_groups=mesh['src'=32,'tgt'=16] {'src'}, use_global_device_ids=true, to_apply=%region_7.8 | all-reduce | flops 1024 | bytes 8192 | tf_op jit(solution)/shard_map/psum | solution.py:75
  214.6 40.4 %while.88 = (s32[]{:T(128)}, f32[1024]{0:T(1024)S(1)}, s32[]{:T(128)}, s32[12]{0:T(128)S(1)}, bf16[1024,512]{1,0:T(8,128)(2,1)S(1)}, /*index=5*/bf16[1024,512]{1...) while((s32[]{:T(128)}, f32[1024]{0:T(1024)S(1)}, ...), condition=%wide.region_9.10_spmd, body=%wide.region_8.9_spmd.sunk | while | flops 67961120 | bytes 1056242 | solution.py:60
  255.1 38.7 %psum.44 = f32[1024]{0:T(1024)S(1)} all-reduce(f32[1024]{0:T(1024)S(1)} %get-tuple-element.682), channel_id=1, replica_groups=mesh['src'=32,'tgt'=16] {'tgt'}, use_global_device_ids=true, to_apply=%region_10.11 | all-reduce | flops 1024 | bytes 8192 | tf_op jit(solution)/shard_map/psum | solution.py:59
  293.8 39.6 %while.89 = (s32[]{:T(128)}, f32[1024]{0:T(1024)S(1)}, s32[]{:T(128)}, s32[12]{0:T(128)S(1)}, f32[1024]{0:T(1024)S(1)}, /*index=5*/bf16[1024,512]{1,0:T(8,128)(2...) while((s32[]{:T(128)}, f32[1024]{0:T(1024)S(1)}, ...), condition=%wide.region_12.13_spmd, body=%wide.region_11.12_spmd.sunk | while | flops 67961120 | bytes 1056242 | solution.py:76
  333.5 67.2 %psum.45 = f32[1024]{0:T(1024)S(1)} all-reduce(f32[1024]{0:T(1024)S(1)} %get-tuple-element.683), channel_id=1, replica_groups=mesh['src'=32,'tgt'=16] {'src'}, use_global_device_ids=true, to_apply=%region_13.14 | all-reduce | flops 1024 | bytes 8192 | tf_op jit(solution)/shard_map/psum | solution.py:75
  400.6 40.5 %while.90 = (s32[]{:T(128)}, f32[1024]{0:T(1024)S(1)}, s32[]{:T(128)}, s32[12]{0:T(128)S(1)}, bf16[1024,512]{1,0:T(8,128)(2,1)S(1)}, /*index=5*/bf16[1024,512]{1...) while((s32[]{:T(128)}, f32[1024]{0:T(1024)S(1)}, ...), condition=%wide.region_15.16_spmd, body=%wide.region_14.15_spmd.sunk | while | flops 67961120 | bytes 1056242 | solution.py:60
  441.1 34.7 %psum.46 = f32[1024]{0:T(1024)S(1)} all-reduce(f32[1024]{0:T(1024)S(1)} %get-tuple-element.684), channel_id=1, replica_groups=mesh['src'=32,'tgt'=16] {'tgt'}, use_global_device_ids=true, to_apply=%region_16.17 | all-reduce | flops 1024 | bytes 8192 | tf_op jit(solution)/shard_map/psum | solution.py:59
  475.9 39.6 %while.91 = (s32[]{:T(128)}, f32[1024]{0:T(1024)S(1)}, s32[]{:T(128)}, s32[12]{0:T(128)S(1)}, f32[1024]{0:T(1024)S(1)}, /*index=5*/bf16[1024,512]{1,0:T(8,128)(2...) while((s32[]{:T(128)}, f32[1024]{0:T(1024)S(1)}, ...), condition=%wide.region_18.19_spmd, body=%wide.region_17.18_spmd.sunk | while | flops 67961120 | bytes 1056242 | solution.py:76
  515.5 77.1 %psum.47 = f32[1024]{0:T(1024)S(1)} all-reduce(f32[1024]{0:T(1024)S(1)} %get-tuple-element.685), channel_id=1, replica_groups=mesh['src'=32,'tgt'=16] {'src'}, use_global_device_ids=true, to_apply=%region_19.20 | all-reduce | flops 1024 | bytes 8192 | tf_op jit(solution)/shard_map/psum | solution.py:75
  594.2 53.3 %while.92 = (s32[]{:T(128)}, f32[1024,512]{1,0:T(8,128)}, f32[1024]{0:T(1024)S(1)}, s32[]{:T(128)}, s32[12]{0:T(128)S(1)}, /*index=5*/bf16[1024,512]{1,0:T(8,128...) while((s32[]{:T(128)}, f32[1024,512]{1,0:T(8,128)}, ...), condition=%wide.region_22.23_spmd, body=%wide.region_20.22_spmd.sunk | while | flops 134610976 | bytes 2104842 | solution.py:99
  605.0 2.2 fusion.143
  618.1 2.2 fusion.143
  631.3 2.2 fusion.143
  644.4 2.2 fusion.143
  647.4 6.9 scatter_custom_fusion
  654.4 4.3 scatter_custom_fusion.2
  658.7 4.3 scatter_custom_fusion.1
  664.9 33.3 %all-reduce = f32[1024]{0:T(1024)S(1)} all-reduce(f32[1024]{0:T(1024)S(1)} %scatter_custom_fusion.1), channel_id=3, replica_groups=mesh['src'=32,'tgt'=16] {'tgt'}, use_global_device_ids=true, to_apply=%region_26.27.clone | all-reduce | flops 1024 | bytes 8192
  698.8 72.2 %reduce-scatter.2.cloned.1.call-done = f32[64,512]{1,0:T(8,128)} async-done(((f32[1024,512]{1,0:T(8,128)}), f32[64,512]{1,0:T(8,128)}) %reduce-scatter.2.cloned.1.call-update) | async-done | bytes 131088 | tf_op jit(solution)/shard_map/reduce_scatter | solution.py:106
  (303 shorter events, 96.3 us)
Async XLA Ops:
  7.2 1.2 copy-start
  7.2 763.8 %reduce-scatter.2.cloned.1.call-start = ((), (), s32[]{:S(2)}) async-start(), calls=%async_computation.1 | async-start | bytes 2228224 | tf_op jit(solution)/shard_map/reduce_scatter | solution.py:106
  8.4 6.6 copy-start.2
  13.5 1.8 copy-start.1
  19.9 2.1 copy-start.4
  102.5 112.1 %copy-start.3 = (f32[1024]{0:T(1024)S(1)}, f32[1024]{0:T(1024)}, u32[]{:S(2)}) copy-start(f32[1024]{0:T(1024)} %param.24) | copy-start | bytes 12292
Sparse Core Ops, SparseCore 0:
  654.5 116.5 reduce-scatter.1
where the time goes:
time: 794 us; the launch traced here: 779 us
  blocking collectives  364 us (46%)
  loops' own time  198 us (25%)
  waiting for transfers between devices  72.2 us (9%)
  local copies, waits for them, and re-layouts  68.8 us (9%)
  matrix products  43.6 us (5%)
  other arithmetic  17.8 us (2%)
  between operations  14.9 us (2%)
    psum x3, blocking collectives, body(): lax.psum(lax.fori_loop(0, tile_total, col_add_tile, jnp.zeros((tgt_count,...  217 us
    psum x3, blocking collectives, body(): lax.psum(lax.fori_loop(0, tile_total, row_add_tile, jnp.zeros((src_count,...  114 us
    another operation x3, loops' own time, body(): lax.fori_loop(0, tile_total, col_add_tile, jnp.zeros((tgt_count,), jnp.fl...  85.5 us
    another operation x3, loops' own time, body(): lax.fori_loop(0, tile_total, row_add_tile, jnp.zeros((src_count,), jnp.fl...  85.5 us
    reduce_scatter x1, waiting for transfers between devices, body(): lax.psum_scatter(numerator, 'tgt', scatter_dimension=0, tiled=True)  72.2 us
    dynamic_slice x56, local copies, waits for them, and re-layouts, make_tile(): code_now = tile_codes[tile_slot]  36.7 us
    unnamed x1, blocking collectives  33.3 us
    another operation x1, loops' own time, body(): numerator, row_mass = lax.fori_loop(0, tile_total, add_projection, empty)  27 us
  transfers between devices with their start and end apart: 1, of which 1 were waited for; matrix products, arithmetic and copies ran while one was open for 1% of the time, Pallas kernels for 0%

commit v1 on v0

v1 whole, which is shorter than its diff:
```python
import functools

import jax
import jax.numpy as jnp
from jax import lax
from jax.experimental import pallas as pl
from jax.experimental.pallas import tpu as pltpu
from jax.sharding import PartitionSpec as P

EMB = 512
BLK = 256
ROWS = 1024
COLS = 1024
ITERS = 3
INVERSE_TEMP = 64.0
MASS_POWER = 0.8
NORM_EPSILON = 1e-06
SHARPNESS = INVERSE_TEMP / EMB
SLOTS = 12
OUT = 64
MESH = pl.DeviceIdType.MESH


def normalize_into(cells, hat):
    def step(i, carry):
        rows = pl.ds(i * BLK, BLK)
        wide = cells[rows, :].astype(jnp.float32)
        mean = jnp.sum(wide * wide, axis=1, keepdims=True) * (1.0 / EMB)
        hat[rows, :] = (wide * lax.rsqrt(mean + NORM_EPSILON)).astype(jnp.bfloat16)
        return carry

    lax.fori_loop(0, ROWS // BLK, step, 0)


def power(x):
    return jnp.exp(MASS_POWER * jnp.log(x))


def as_row(tile):
    return jnp.concatenate([tile[k : k + 1, :] for k in range(8)], axis=1)


def split_rows(tile):
    which = lax.broadcasted_iota(jnp.int32, (8, 128), 0)
    pieces = []
    for k in range(8):
        value = jnp.broadcast_to(tile[k : k + 1, :], (8, 128))
        high = value.astype(jnp.bfloat16).astype(jnp.float32)
        piece = jnp.where(which == 0, high, jnp.where(which == 1, value - high, 0.0))
        pieces.append(piece.astype(jnp.bfloat16))
    return jnp.concatenate(pieces, axis=1)


def as_tile(rows):
    which = lax.broadcasted_iota(jnp.int32, (8, 128), 0)
    tile = jnp.zeros((8, 128), jnp.float32)
    for k in range(8):
        piece = jnp.sum(rows[:, k * 128 : (k + 1) * 128], axis=0, keepdims=True)
        tile = jnp.where(which == k, piece, tile)
    return tile


def kernel(
    n_z,
    src_ref,
    tgt_ref,
    smass_ref,
    tmass_ref,
    order_ref,
    list_ref,
    count_ref,
    proj_ref,
    log_ref,
    src_hat,
    tgt_hat,
    k_wide,
    k_half,
    scaled,
    outbox,
    plane_in,
    z_in,
    core_in,
    num,
    relay_p,
    relay_m,
    from_m,
    from_p,
    relay2_p,
    relay2_m,
    from2_m,
    from2_p,
    small_send,
    small_recv,
    big_send,
    big_recv,
):
    s = lax.axis_index("src")
    t = lax.axis_index("tgt")
    z = s // 2
    core = s % 2
    y = t // 4
    x = t % 4

    plane_steps = [(dy, dx) for dy in range(4) for dx in range(4) if (dy, dx) != (0, 0)]
    plane_steps.sort(key=lambda d: -(min(d[0], 4 - d[0]) + min(d[1], 4 - d[1])))
    plane_peers = [(s, ((y + dy) % 4) * 4 + (x + dx) % 4) for dy, dx in plane_steps]
    z_steps = sorted(range(1, n_z), key=lambda d: -min(d, n_z - d))
    z_peers = [(((z + d) % n_z) * 2 + core, t) for d in z_steps]
    sibling = (z * 2 + 1 - core, t)

    def device(where):
        return {"src": where[0], "tgt": where[1]}

    barrier = pltpu.get_barrier_semaphore()
    everyone = z_peers + plane_peers + [sibling]
    for where in everyone:
        pl.semaphore_signal(barrier, 1, device_id=device(where), device_id_type=MESH)

    bits = jnp.int32(0)
    total = count_ref[0, 0]
    for slot in range(SLOTS):
        code = jnp.maximum(list_ref[0, slot], 0)
        bits = bits | jnp.where(slot < total, jnp.int32(1) << code, 0)
    position = lax.broadcasted_iota(jnp.int32, (1, ROWS), 1)
    bits_row = jnp.full((1, ROWS), bits, jnp.int32)
    nibble = (lax.shift_right_logical(bits_row, (position // BLK) * 4) & 15).astype(jnp.float32)

    normalize_into(src_ref, src_hat)
    normalize_into(tgt_ref, tgt_hat)

    def build(i, carry):
        rows = pl.ds(i * BLK, BLK)
        row_ids = lax.broadcasted_iota(jnp.int32, (BLK, 1), 0) + i * BLK
        placed = jnp.where(order_ref[...] == row_ids, nibble, 0.0)
        links = jnp.sum(placed, axis=1, keepdims=True).astype(jnp.int32)
        for q in range(COLS // BLK):
            cols = pl.ds(q * BLK, BLK)
            similarity = lax.dot_general(
                src_hat[rows, :],
                tgt_hat[cols, :],
                (((1,), (1,)), ((), ())),
                preferred_element_type=jnp.float32,
            )
            linked = (lax.shift_right_logical(links, q) & 1).astype(jnp.float32)
            tile = jnp.exp(similarity * SHARPNESS) * linked
            k_wide[rows, cols] = tile
            k_half[rows, cols] = tile.astype(jnp.bfloat16)
        return carry

    lax.fori_loop(0, ROWS // BLK, build, 0)

    def row_product(tile):
        return as_tile(
            lax.dot_general(
                split_rows(tile),
                k_half[...],
                (((1,), (1,)), ((), ())),
                preferred_element_type=jnp.float32,
            )
        )

    def col_product(tile):
        return as_tile(
            jnp.dot(split_rows(tile), k_half[...], preferred_element_type=jnp.float32)
        )

    def broadcast(box, inbox, peers, sem):
        for slot, where in enumerate(peers):
            pltpu.make_async_remote_copy(
                src_ref=outbox.at[box],
                dst_ref=inbox.at[slot],
                send_sem=small_send.at[sem],
                recv_sem=small_recv.at[sem],
                device_id=device(where),
                device_id_type=MESH,
            ).start()

    def arrived(inbox, sem):
        pltpu.make_async_copy(inbox, inbox, small_recv.at[sem]).wait()

    def sent(inbox, sem):
        pltpu.make_async_copy(inbox, inbox, small_send.at[sem]).wait()

    tgt_scale = jnp.ones((8, 128), jnp.float32)
    src_scale = jnp.ones((8, 128), jnp.float32)
    pl.semaphore_wait(barrier, len(everyone))
    for i in range(ITERS):
        mine = row_product(tgt_scale)
        outbox[3 * i] = mine
        broadcast(3 * i, plane_in.at[i], plane_peers, 3 * i)
        arrived(plane_in.at[i], 3 * i)
        src_scale = power(smass_ref[...] / (mine + jnp.sum(plane_in[i], axis=0)))

        mine = col_product(src_scale)
        outbox[3 * i + 1] = mine
        broadcast(3 * i + 1, z_in.at[i], z_peers, 3 * i + 1)
        arrived(z_in.at[i], 3 * i + 1)
        mine = mine + jnp.sum(z_in[i], axis=0)
        outbox[3 * i + 2] = mine
        broadcast(3 * i + 2, core_in.at[i], [sibling], 3 * i + 2)
        arrived(core_in.at[i], 3 * i + 2)
        tgt_scale = power(tmass_ref[...] / (mine + core_in[i, 0]))

    a = jnp.where(core == 0, x, y)
    b = jnp.where(core == 0, y, x)
    step_a = 1 + 3 * core
    step_b = 4 - 3 * core

    def at(a_now, b_now):
        return (s, (a_now % 4) * step_a + (b_now % 4) * step_b)

    tgt_row = as_row(tgt_scale)

    def numerators(d):
        for e in range(4):
            chunk = ((a + d) % 4) * step_a + e * step_b
            weighted = k_wide[pl.ds(chunk * OUT, OUT), :] * tgt_row
            scaled[e * OUT : (e + 1) * OUT, :] = weighted.astype(jnp.bfloat16)
        num[d] = jnp.dot(
            scaled[...], tgt_ref[...], preferred_element_type=jnp.float32
        ).reshape(4, OUT, EMB)

    def send(src, dst, where, sem):
        copy = pltpu.make_async_remote_copy(
            src_ref=src,
            dst_ref=dst,
            send_sem=big_send.at[sem],
            recv_sem=big_recv.at[sem],
            device_id=device(where),
            device_id_type=MESH,
        )
        copy.start()
        return copy

    a_next, a_last = at(a + 1, b), at(a - 1, b)
    b_next, b_last = at(a, b + 1), at(a, b - 1)
    numerators(2)
    first_p = send(num.at[2, 0:2], relay_p, a_next, 0)
    first_m = send(num.at[2, 2:4], relay_m, a_last, 1)
    numerators(1)
    direct_p = send(num.at[1, 2:4], from_m.at[2:4], a_next, 2)
    numerators(3)
    direct_m = send(num.at[3, 0:2], from_p.at[0:2], a_last, 3)

    mass = row_product(tgt_scale)
    outbox[9] = mass
    broadcast(9, plane_in.at[3], plane_peers, 9)

    first_p.wait_recv()
    num[1, 0:2] = num[1, 0:2] + relay_p[...]
    second_p = send(num.at[1, 0:2], from_m.at[0:2], a_next, 4)
    first_m.wait_recv()
    num[3, 2:4] = num[3, 2:4] + relay_m[...]
    second_m = send(num.at[3, 2:4], from_p.at[2:4], a_last, 5)
    numerators(0)
    direct_p.wait_recv()
    direct_m.wait_recv()
    second_p.wait_recv()
    second_m.wait_recv()
    num[0] = num[0] + from_m[...] + from_p[...]

    half = OUT // 2
    up, down, over = (b + 1) % 4, (b + 3) % 4, (b + 2) % 4
    far_p = send(num.at[0, over, 0:half], relay2_p, b_next, 6)
    far_m = send(num.at[0, over, half:OUT], relay2_m, b_last, 7)
    near_p = send(num.at[0, up, half:OUT], from2_m.at[half:OUT], b_next, 8)
    near_m = send(num.at[0, down, 0:half], from2_p.at[0:half], b_last, 9)
    far_p.wait_recv()
    num[0, up, 0:half] = num[0, up, 0:half] + relay2_p[...]
    last_p = send(num.at[0, up, 0:half], from2_m.at[0:half], b_next, 10)
    far_m.wait_recv()
    num[0, down, half:OUT] = num[0, down, half:OUT] + relay2_m[...]
    last_m = send(num.at[0, down, half:OUT], from2_p.at[half:OUT], b_last, 11)

    arrived(plane_in.at[3], 9)
    mass = mass + jnp.sum(plane_in[3], axis=0)
    logs = jnp.log(src_scale) + jnp.log(mass)
    sub = lax.broadcasted_iota(jnp.int32, (8, 128), 0)
    mine_now = sub == t // 2
    log_row = jnp.sum(jnp.where(mine_now, logs, 0.0), axis=0, keepdims=True)
    mass_row = jnp.sum(jnp.where(mine_now, mass, 0.0), axis=0, keepdims=True)
    odd = jnp.full((1, OUT), t % 2, jnp.int32) == 1
    log_ref[...] = jnp.where(odd, log_row[:, OUT:], log_row[:, :OUT])
    row_id = lax.broadcasted_iota(jnp.int32, (OUT, 128), 0) + (t % 2) * OUT
    lane_id = lax.broadcasted_iota(jnp.int32, (OUT, 128), 1)
    mass_col = jnp.sum(jnp.where(row_id == lane_id, mass_row, 0.0), axis=1, keepdims=True)

    near_p.wait_recv()
    near_m.wait_recv()
    last_p.wait_recv()
    last_m.wait_recv()
    final = num[0, b] + from2_m[...] + from2_p[...]
    proj_ref[...] = (final / mass_col).astype(jnp.bfloat16)

    for i in range(ITERS):
        sent(plane_in.at[i], 3 * i)
        sent(z_in.at[i], 3 * i + 1)
        sent(core_in.at[i], 3 * i + 2)
    sent(plane_in.at[3], 9)
    for copy in (first_p, first_m, direct_p, direct_m, second_p, second_m):
        copy.wait_send()
    for copy in (far_p, far_m, near_p, near_m, last_p, last_m):
        copy.wait_send()


def body(n_z, source_cells, target_cells, source_mass, target_mass, source_order, tile_list, tile_count):
    vmem = pl.BlockSpec(memory_space=pltpu.VMEM)
    smem = pl.BlockSpec(memory_space=pltpu.SMEM)
    half = OUT // 2
    f32, bf16 = jnp.float32, jnp.bfloat16
    projected, log_mass = pl.pallas_call(
        functools.partial(kernel, n_z),
        out_shape=(
            jax.ShapeDtypeStruct((OUT, EMB), bf16),
            jax.ShapeDtypeStruct((1, OUT), f32),
        ),
        in_specs=[vmem] * 5 + [smem] * 2,
        out_specs=(vmem, vmem),
        scratch_shapes=[
            pltpu.VMEM((ROWS, EMB), bf16),
            pltpu.VMEM((COLS, EMB), bf16),
            pltpu.VMEM((ROWS, COLS), f32),
            pltpu.VMEM((ROWS, COLS), bf16),
            pltpu.VMEM((BLK, COLS), bf16),
            pltpu.VMEM((10, 8, 128), f32),
            pltpu.VMEM((4, 15, 8, 128), f32),
            pltpu.VMEM((3, n_z - 1, 8, 128), f32),
            pltpu.VMEM((3, 1, 8, 128), f32),
            pltpu.VMEM((4, 4, OUT, EMB), f32),
            pltpu.VMEM((2, OUT, EMB), f32),
            pltpu.VMEM((2, OUT, EMB), f32),
            pltpu.VMEM((4, OUT, EMB), f32),
            pltpu.VMEM((4, OUT, EMB), f32),
            pltpu.VMEM((half, EMB), f32),
            pltpu.VMEM((half, EMB), f32),
            pltpu.VMEM((OUT, EMB), f32),
            pltpu.VMEM((OUT, EMB), f32),
            pltpu.SemaphoreType.DMA((10,)),
            pltpu.SemaphoreType.DMA((10,)),
            pltpu.SemaphoreType.DMA((12,)),
            pltpu.SemaphoreType.DMA((12,)),
        ],
        compiler_params=pltpu.CompilerParams(
            collective_id=0, has_side_effects=True, vmem_limit_bytes=48 * 1024 * 1024
        ),
    )(
        source_cells,
        target_cells,
        source_mass.reshape(8, 128),
        target_mass.reshape(8, 128),
        source_order.reshape(1, ROWS),
        tile_list,
        tile_count,
    )
    return projected, log_mass.reshape(OUT)


def solution(mesh):
    placed = (
        P("src", None),
        P("tgt", None),
        P("src"),
        P("tgt"),
        P("src"),
        P("src", "tgt"),
        P("src", "tgt"),
    )
    return jax.shard_map(
        functools.partial(body, mesh.shape["src"] // 2),
        mesh=mesh,
        in_specs=placed,
        out_specs=(P(("src", "tgt"), None), P(("src", "tgt"))),
        check_vma=False,
    )
```

time: 794 us -> 82.7 us (0.10); the launches traced: 779 us -> 82.4 us
  blocking collectives: 364 us -> 0 us
  loops' own time: 198 us -> 0 us
  Pallas kernels: 0 us -> 75.5 us
  waiting for transfers between devices: 72.2 us -> 0 us
  local copies, waits for them, and re-layouts: 68.8 us -> 5.61 us
  matrix products: 43.6 us -> 0 us
  other arithmetic: 17.8 us -> 0 us
  between operations: 14.9 us -> 1.32 us
    psum x6 -> x0, blocking collectives: 331 us -> none  [the longest x3 217 us: body(): lax.psum(lax.fori_loop(0, tile_total, col_add_tile, jnp.zeros((tgt_count,...]
    another operation x7 -> x0, loops' own time: 198 us -> none  [the longest x3 85.5 us: body(): lax.fori_loop(0, tile_total, col_add_tile, jnp.zeros((tgt_count,), jnp.fl...]
    pallas_call x0 -> x1, Pallas kernels: none -> 75.5 us  [body(): pl.pallas_call(functools.partial(kernel, n_z), out_shape=(jax.ShapeDtypeS...]
    reduce_scatter x1 -> x0, waiting for transfers between devices: 72.2 us -> none  [body(): lax.psum_scatter(numerator, 'tgt', scatter_dimension=0, tiled=True)]
    dot_general x112 -> x0, matrix products: 43.6 us -> none  [the longest x8 17.5 us: add_projection(): jnp.dot(weighted.astype(jnp.bfloat16), tgt_rows, preferred_element_type=j...]
    dynamic_slice x104 -> x0, local copies, waits for them, and re-layouts: 40.4 us -> none  [the longest x56 36.7 us: make_tile(): code_now = tile_codes[tile_slot]]
    unnamed x1 -> x0, blocking collectives: 33.3 us -> none
    scatter x3 -> x0, local copies, waits for them, and re-layouts: 15.5 us -> none  [the longest x1 6.9 us: body(): numerator = jnp.zeros_like(numerator).at[source_order].set(numerator)]
  transfers between devices with their start and end apart: 1 -> 0, of which waited for: 1 -> 0; matrix products, arithmetic and copies ran while one was open for 1% -> 0% of each run, Pallas kernels for 0% -> 0%
where the time goes in v1:
time: 82.7 us; the launch traced here: 82.4 us
  Pallas kernels  75.5 us (91%)
  local copies, waits for them, and re-layouts  5.61 us (7%)
  between operations  1.32 us (2%)
    pallas_call x1, Pallas kernels, body(): pl.pallas_call(functools.partial(kernel, n_z), out_shape=(jax.ShapeDtypeS...  75.5 us
    unnamed x14, local copies, waits for them, and re-layouts  5.61 us

profile of v1, /device:TPU:1, one launch (start us, length us, event | category | flops | bytes accessed | tf_op | source)
XLA Modules:
  0.0 82.4 jit_solution(7101624417099707867)
XLA Ops:
  0.6 0.0 copy-start.2
  1.3 0.0 copy-start.5
  1.3 0.0 copy-done.2
  1.3 0.6 copy-done.5
  2.0 0.0 copy-start
  2.0 1.2 %copy-done = bf16[1024,512]{1,0:T(8,128)(2,1)S(1)} copy-done((bf16[1024,512]{1,0:T(8,128)(2,1)S(1)}, bf16[1024,512]{1,0:T(8,128)(2,1)}, u32[]{:S(2)}) %copy-start) | copy-done | bytes 1048600
  3.2 0.0 copy-start.1
  3.2 1.2 %copy-done.1 = bf16[1024,512]{1,0:T(8,128)(2,1)S(1)} copy-done((bf16[1024,512]{1,0:T(8,128)(2,1)S(1)}, bf16[1024,512]{1,0:T(8,128)(2,1)}, u32[]{:S(2)}) %copy-start.1) | copy-done | bytes 1048600
  4.4 0.0 copy-start.3
  4.4 0.7 copy-done.3
  5.1 0.0 copy-start.4
  5.1 0.7 copy-done.4
  5.8 75.5 %shard_map.86 = (bf16[64,512]{1,0:T(8,128)(2,1)S(1)}, f32[1,64]{1,0:T(1,128)S(1)}) custom-call(bf16[1024,512]{1,0:T(8,128)(2,1)S(1)} %copy-done, bf16[1024,512]{1,0:T(8,128)(2,1)S(1)} %copy-done.1, f32[8,128]{1,0:T(8,128)S(1)} %bitcast.4, f32[8,128]{1,0:T(8,128)S(1)} %bitcast.5, s32[1,1024]{1,0:T(1,128)S(1)} %bitcast.6, s32[1,12]{1,0:T(1,128)S(1)} %copy-done.5, ...), custom_call_target="tpu_custom_call" | custom-call | tf_op jit(solution)/shard_map/pallas_call | solution.py:311
  81.2 0.6 copy.12
  81.9 0.5 copy.13
Async XLA Ops:
  0.6 0.7 copy-start.2
  1.3 0.7 copy-start.5
  2.0 1.2 %copy-start = (bf16[1024,512]{1,0:T(8,128)(2,1)S(1)}, bf16[1024,512]{1,0:T(8,128)(2,1)}, u32[]{:S(2)}) copy-start(bf16[1024,512]{1,0:T(8,128)(2,1)} %src_ref.1) | copy-start | bytes 3145732
  3.2 1.2 %copy-start.1 = (bf16[1024,512]{1,0:T(8,128)(2,1)S(1)}, bf16[1024,512]{1,0:T(8,128)(2,1)}, u32[]{:S(2)}) copy-start(bf16[1024,512]{1,0:T(8,128)(2,1)} %tgt_ref.1) | copy-start | bytes 3145732
  4.4 0.7 copy-start.3
  5.1 0.7 copy-start.4

commit v2 on v1

v2 whole, which is shorter than its diff:
```python
import functools

import jax
import jax.numpy as jnp
from jax import lax
from jax.experimental import pallas as pl
from jax.experimental.pallas import tpu as pltpu
from jax.sharding import PartitionSpec as P

EMB = 512
BLK = 256
ROWS = 1024
COLS = 1024
ITERS = 3
INVERSE_TEMP = 64.0
MASS_POWER = 0.8
NORM_EPSILON = 1e-06
SHARPNESS = INVERSE_TEMP / EMB
SLOTS = 12
OUT = 64
WIDE = EMB // 2
FAR = 8
MESH = pl.DeviceIdType.MESH


def normalize_into(cells, hat):
    def step(i, carry):
        rows = pl.ds(i * BLK, BLK)
        wide = cells[rows, :].astype(jnp.float32)
        mean = jnp.sum(wide * wide, axis=1, keepdims=True) * (1.0 / EMB)
        hat[rows, :] = (wide * lax.rsqrt(mean + NORM_EPSILON)).astype(jnp.bfloat16)
        return carry

    lax.fori_loop(0, ROWS // BLK, step, 0)


def power(x):
    return jnp.exp(MASS_POWER * jnp.log(x))


def as_row(tile):
    return jnp.concatenate([tile[k : k + 1, :] for k in range(8)], axis=1)


def split_rows(tile):
    which = lax.broadcasted_iota(jnp.int32, (8, 128), 0)
    pieces = []
    for k in range(8):
        value = jnp.broadcast_to(tile[k : k + 1, :], (8, 128))
        high = value.astype(jnp.bfloat16).astype(jnp.float32)
        piece = jnp.where(which == 0, high, jnp.where(which == 1, value - high, 0.0))
        pieces.append(piece.astype(jnp.bfloat16))
    return jnp.concatenate(pieces, axis=1)


def as_tile(rows):
    which = lax.broadcasted_iota(jnp.int32, (8, 128), 0)
    tile = jnp.zeros((8, 128), jnp.float32)
    for k in range(8):
        piece = jnp.sum(rows[:, k * 128 : (k + 1) * 128], axis=0, keepdims=True)
        tile = jnp.where(which == k, piece, tile)
    return tile


def kernel(
    n_z,
    src_hbm,
    tgt_hbm,
    smass_hbm,
    tmass_hbm,
    order_hbm,
    list_hbm,
    proj_ref,
    log_ref,
    src_ref,
    tgt_ref,
    smass_ref,
    tmass_ref,
    order_ref,
    list_ref,
    src_hat,
    tgt_hat,
    k_wide,
    k_half,
    k_turned,
    scaled,
    outbox,
    plane_in,
    far_in,
    near_in,
    core_in,
    num,
    relay_p,
    relay_m,
    from_m,
    from_p,
    relay2_p,
    relay2_m,
    from2_m,
    from2_p,
    over2,
    load_sem,
    small_send,
    small_recv,
    big_send,
    big_recv,
):
    s = lax.axis_index("src")
    t = lax.axis_index("tgt")
    z = s // 2
    core = s % 2
    y = t // 4
    x = t % 4

    plane_steps = [(dy, dx) for dy in range(4) for dx in range(4) if (dy, dx) != (0, 0)]
    plane_steps.sort(key=lambda d: -(min(d[0], 4 - d[0]) + min(d[1], 4 - d[1])))
    plane_peers = [(s, ((y + dy) % 4) * 4 + (x + dx) % 4) for dy, dx in plane_steps]
    z_steps = sorted(range(1, n_z), key=lambda d: -min(d, n_z - d))
    far_steps = [d for d in z_steps if min(d, n_z - d) >= FAR]
    near_steps = [d for d in z_steps if min(d, n_z - d) < FAR]
    far_peers = [
        (((z + d) % n_z) * 2 + side, t) for d in far_steps for side in (core, 1 - core)
    ]
    near_peers = [(((z + d) % n_z) * 2 + core, t) for d in near_steps]
    sibling = (z * 2 + 1 - core, t)

    def device(where):
        return {"src": where[0], "tgt": where[1]}

    barrier = pltpu.get_barrier_semaphore()
    everyone = far_peers + near_peers + plane_peers + [sibling]
    for where in everyone:
        pl.semaphore_signal(barrier, 1, device_id=device(where), device_id_type=MESH)
    loads = [
        pltpu.make_async_copy(there, here, load_sem.at[i])
        for i, (there, here) in enumerate(
            (
                (src_hbm, src_ref),
                (tgt_hbm, tgt_ref),
                (order_hbm, order_ref),
                (list_hbm, list_ref),
                (smass_hbm, smass_ref),
                (tmass_hbm, tmass_ref),
            )
        )
    ]
    for load in loads:
        load.start()
    loads[0].wait()
    normalize_into(src_ref, src_hat)
    loads[1].wait()
    normalize_into(tgt_ref, tgt_hat)
    for load in loads[2:]:
        load.wait()

    codes = jnp.maximum(list_ref[...], 0)
    live = list_ref[...] >= 0
    flags = jnp.where(live, jnp.int32(1) << codes, 0).astype(jnp.float32)
    bits = jnp.sum(flags, axis=1, keepdims=True).astype(jnp.int32)
    position = lax.broadcasted_iota(jnp.int32, (1, ROWS), 1)
    bits_row = jnp.broadcast_to(bits, (1, ROWS))
    nibble = (lax.shift_right_logical(bits_row, (position // BLK) * 4) & 15).astype(jnp.float32)

    def build(i, carry):
        rows = pl.ds(i * BLK, BLK)
        row_ids = lax.broadcasted_iota(jnp.int32, (BLK, 1), 0) + i * BLK
        placed = jnp.where(order_ref[...] == row_ids, nibble, 0.0)
        links = jnp.sum(placed, axis=1, keepdims=True).astype(jnp.int32)
        for q in range(COLS // BLK):
            cols = pl.ds(q * BLK, BLK)
            similarity = lax.dot_general(
                src_hat[rows, :],
                tgt_hat[cols, :],
                (((1,), (1,)), ((), ())),
                preferred_element_type=jnp.float32,
            )
            linked = (lax.shift_right_logical(links, q) & 1).astype(jnp.float32)
            tile = jnp.exp(similarity * SHARPNESS) * linked
            k_wide[rows, cols] = tile
            k_half[rows, cols] = tile.astype(jnp.bfloat16)
        return carry

    lax.fori_loop(0, ROWS // BLK, build, 0)

    def turn(i, carry):
        rows = pl.ds(i * BLK, BLK)
        for q in range(COLS // BLK):
            cols = pl.ds(q * BLK, BLK)
            k_turned[cols, rows] = jnp.transpose(k_wide[rows, cols]).astype(jnp.bfloat16)
        return carry

    def first_row_product(tile):
        return as_tile(
            lax.dot_general(
                split_rows(tile),
                k_half[...],
                (((1,), (1,)), ((), ())),
                preferred_element_type=jnp.float32,
            )
        )

    def row_product(tile):
        return as_tile(
            jnp.dot(split_rows(tile), k_turned[...], preferred_element_type=jnp.float32)
        )

    def col_product(tile):
        return as_tile(
            jnp.dot(split_rows(tile), k_half[...], preferred_element_type=jnp.float32)
        )

    def broadcast(box, inbox, peers, sem):
        for slot, where in enumerate(peers):
            pltpu.make_async_remote_copy(
                src_ref=outbox.at[box],
                dst_ref=inbox.at[slot],
                send_sem=small_send.at[sem],
                recv_sem=small_recv.at[sem],
                device_id=device(where),
                device_id_type=MESH,
            ).start()

    def arrived(inbox, sem):
        pltpu.make_async_copy(inbox, inbox, small_recv.at[sem]).wait()

    def sent(inbox, sem):
        pltpu.make_async_copy(inbox, inbox, small_send.at[sem]).wait()

    tgt_scale = jnp.ones((8, 128), jnp.float32)
    src_scale = jnp.ones((8, 128), jnp.float32)
    pl.semaphore_wait(barrier, len(everyone))
    for i in range(ITERS):
        mine = row_product(tgt_scale) if i else first_row_product(tgt_scale)
        outbox[3 * i] = mine
        broadcast(3 * i, plane_in.at[i], plane_peers, 4 * i)
        if i == 0:
            lax.fori_loop(0, ROWS // BLK, turn, 0)
        arrived(plane_in.at[i], 4 * i)
        src_scale = power(smass_ref[...] / (mine + jnp.sum(plane_in[i], axis=0)))

        mine = col_product(src_scale)
        outbox[3 * i + 1] = mine
        broadcast(3 * i + 1, far_in.at[i], far_peers, 4 * i + 1)
        broadcast(3 * i + 1, near_in.at[i], near_peers, 4 * i + 2)
        arrived(near_in.at[i], 4 * i + 2)
        mine = mine + jnp.sum(near_in[i], axis=0)
        outbox[3 * i + 2] = mine
        broadcast(3 * i + 2, core_in.at[i], [sibling], 4 * i + 3)
        arrived(far_in.at[i], 4 * i + 1)
        mine = mine + jnp.sum(far_in[i], axis=0)
        arrived(core_in.at[i], 4 * i + 3)
        tgt_scale = power(tmass_ref[...] / (mine + core_in[i, 0]))

    a = jnp.where(core == 0, x, y)
    b = jnp.where(core == 0, y, x)
    step_a = 1 + 3 * core
    step_b = 4 - 3 * core

    def at(a_now, b_now):
        return (s, (a_now % 4) * step_a + (b_now % 4) * step_b)

    tgt_row = as_row(tgt_scale)

    def scale_rows(d):
        for e in range(4):
            chunk = ((a + d) % 4) * step_a + e * step_b
            weighted = k_wide[pl.ds(chunk * OUT, OUT), :] * tgt_row
            scaled[e * OUT : (e + 1) * OUT, :] = weighted.astype(jnp.bfloat16)

    def numerators(d, h):
        num[h, d] = jnp.dot(
            scaled[...],
            tgt_ref[:, h * WIDE : (h + 1) * WIDE],
            preferred_element_type=jnp.float32,
        ).reshape(4, OUT, WIDE)

    started = []

    def send(src, dst, where):
        sem = len(started)
        copy = pltpu.make_async_remote_copy(
            src_ref=src,
            dst_ref=dst,
            send_sem=big_send.at[sem],
            recv_sem=big_recv.at[sem],
            device_id=device(where),
            device_id_type=MESH,
        )
        copy.start()
        started.append(copy)
        return copy

    a_next, a_last = at(a + 1, b), at(a - 1, b)
    b_next, b_last, b_over = at(a, b + 1), at(a, b - 1), at(a, b + 2)
    first_p, first_m, direct, second = {}, {}, {}, {}
    scale_rows(2)
    for h in range(2):
        numerators(2, h)
        first_p[h] = send(num.at[h, 2, 0:2], relay_p.at[h], a_next)
        first_m[h] = send(num.at[h, 2, 2:4], relay_m.at[h], a_last)
    scale_rows(1)
    for h in range(2):
        numerators(1, h)
        direct[h] = [send(num.at[h, 1, 2:4], from_m.at[h, 2:4], a_next)]
    scale_rows(3)
    for h in range(2):
        numerators(3, h)
        direct[h].append(send(num.at[h, 3, 0:2], from_p.at[h, 0:2], a_last))

    for h in range(2):
        first_p[h].wait_recv()
        num[h, 1, 0:2] = num[h, 1, 0:2] + relay_p[h]
        second[h] = [send(num.at[h, 1, 0:2], from_m.at[h, 0:2], a_next)]
        first_m[h].wait_recv()
        num[h, 3, 2:4] = num[h, 3, 2:4] + relay_m[h]
        second[h].append(send(num.at[h, 3, 2:4], from_p.at[h, 2:4], a_last))

    mass = row_product(tgt_scale)
    outbox[9] = mass
    broadcast(9, plane_in.at[3], plane_peers, 12)

    scale_rows(0)
    for h in range(2):
        numerators(0, h)

    def gather(h):
        for copy in direct[h] + second[h]:
            copy.wait_recv()
        num[h, 0] = num[h, 0] + from_m[h] + from_p[h]

    half = OUT // 2
    up, down, over = (b + 1) % 4, (b + 3) % 4, (b + 2) % 4
    gather(0)
    far_p = send(num.at[0, 0, over, 0:half], relay2_p, b_next)
    far_m = send(num.at[0, 0, over, half:OUT], relay2_m, b_last)
    ends = [
        send(num.at[0, 0, up, half:OUT], from2_m.at[0, half:OUT], b_next),
        send(num.at[0, 0, down, 0:half], from2_p.at[0, 0:half], b_last),
    ]
    gather(1)
    ends.append(send(num.at[1, 0, over], over2, b_over))
    ends.append(send(num.at[1, 0, up], from2_m.at[1], b_next))
    ends.append(send(num.at[1, 0, down], from2_p.at[1], b_last))
    far_p.wait_recv()
    num[0, 0, up, 0:half] = num[0, 0, up, 0:half] + relay2_p[...]
    ends.append(send(num.at[0, 0, up, 0:half], from2_m.at[0, 0:half], b_next))
    far_m.wait_recv()
    num[0, 0, down, half:OUT] = num[0, 0, down, half:OUT] + relay2_m[...]
    ends.append(send(num.at[0, 0, down, half:OUT], from2_p.at[0, half:OUT], b_last))

    arrived(plane_in.at[3], 12)
    mass = mass + jnp.sum(plane_in[3], axis=0)
    logs = jnp.log(src_scale) + jnp.log(mass)
    sub = lax.broadcasted_iota(jnp.int32, (8, 128), 0)
    mine_now = sub == t // 2
    log_row = jnp.sum(jnp.where(mine_now, logs, 0.0), axis=0, keepdims=True)
    mass_row = jnp.sum(jnp.where(mine_now, mass, 0.0), axis=0, keepdims=True)
    odd = jnp.full((1, OUT), t % 2, jnp.int32) == 1
    log_ref[...] = jnp.where(odd, log_row[:, OUT:], log_row[:, :OUT])
    row_id = lax.broadcasted_iota(jnp.int32, (OUT, 128), 0) + (t % 2) * OUT
    lane_id = lax.broadcasted_iota(jnp.int32, (OUT, 128), 1)
    mass_col = jnp.sum(jnp.where(row_id == lane_id, mass_row, 0.0), axis=1, keepdims=True)

    for copy in ends:
        copy.wait_recv()
    final = num[0, 0, b] + from2_m[0] + from2_p[0]
    proj_ref[:, 0:WIDE] = (final / mass_col).astype(jnp.bfloat16)
    final = num[1, 0, b] + from2_m[1] + from2_p[1] + over2[...]
    proj_ref[:, WIDE:EMB] = (final / mass_col).astype(jnp.bfloat16)

    for i in range(ITERS):
        sent(plane_in.at[i], 4 * i)
        sent(far_in.at[i], 4 * i + 1)
        sent(near_in.at[i], 4 * i + 2)
        sent(core_in.at[i], 4 * i + 3)
    sent(plane_in.at[3], 12)
    for copy in started:
        copy.wait_send()


def body(n_z, source_cells, target_cells, source_mass, target_mass, source_order, tile_list, tile_count):
    vmem = pl.BlockSpec(memory_space=pltpu.VMEM)
    hbm = pl.BlockSpec(memory_space=pltpu.HBM)
    half = OUT // 2
    near = len([d for d in range(1, n_z) if min(d, n_z - d) < FAR])
    far = 2 * (n_z - 1 - near)
    f32, bf16, i32 = jnp.float32, jnp.bfloat16, jnp.int32
    projected, log_mass = pl.pallas_call(
        functools.partial(kernel, n_z),
        out_shape=(
            jax.ShapeDtypeStruct((OUT, EMB), bf16),
            jax.ShapeDtypeStruct((1, OUT), f32),
        ),
        in_specs=[hbm] * 6,
        out_specs=(vmem, vmem),
        scratch_shapes=[
            pltpu.VMEM((ROWS, EMB), bf16),
            pltpu.VMEM((COLS, EMB), bf16),
            pltpu.VMEM((8, 128), f32),
            pltpu.VMEM((8, 128), f32),
            pltpu.VMEM((1, ROWS), i32),
            pltpu.VMEM((1, SLOTS), i32),
            pltpu.VMEM((ROWS, EMB), bf16),
            pltpu.VMEM((COLS, EMB), bf16),
            pltpu.VMEM((ROWS, COLS), f32),
            pltpu.VMEM((ROWS, COLS), bf16),
            pltpu.VMEM((COLS, ROWS), bf16),
            pltpu.VMEM((BLK, COLS), bf16),
            pltpu.VMEM((10, 8, 128), f32),
            pltpu.VMEM((4, 15, 8, 128), f32),
            pltpu.VMEM((3, far, 8, 128), f32),
            pltpu.VMEM((3, near, 8, 128), f32),
            pltpu.VMEM((3, 1, 8, 128), f32),
            pltpu.VMEM((2, 4, 4, OUT, WIDE), f32),
            pltpu.VMEM((2, 2, OUT, WIDE), f32),
            pltpu.VMEM((2, 2, OUT, WIDE), f32),
            pltpu.VMEM((2, 4, OUT, WIDE), f32),
            pltpu.VMEM((2, 4, OUT, WIDE), f32),
            pltpu.VMEM((half, WIDE), f32),
            pltpu.VMEM((half, WIDE), f32),
            pltpu.VMEM((2, OUT, WIDE), f32),
            pltpu.VMEM((2, OUT, WIDE), f32),
            pltpu.VMEM((OUT, WIDE), f32),
            pltpu.SemaphoreType.DMA((6,)),
            pltpu.SemaphoreType.DMA((13,)),
            pltpu.SemaphoreType.DMA((13,)),
            pltpu.SemaphoreType.DMA((21,)),
            pltpu.SemaphoreType.DMA((21,)),
        ],
        compiler_params=pltpu.CompilerParams(
            collective_id=0, has_side_effects=True, vmem_limit_bytes=64 * 1024 * 1024
        ),
    )(
        source_cells,
        target_cells,
        source_mass.reshape(8, 128),
        target_mass.reshape(8, 128),
        source_order.reshape(1, ROWS),
        tile_list,
    )
    return projected, log_mass.reshape(OUT)


def solution(mesh):
    placed = (
        P("src", None),
        P("tgt", None),
        P("src"),
        P("tgt"),
        P("src"),
        P("src", "tgt"),
        P("src", "tgt"),
    )
    return jax.shard_map(
        functools.partial(body, mesh.shape["src"] // 2),
        mesh=mesh,
        in_specs=placed,
        out_specs=(P(("src", "tgt"), None), P(("src", "tgt"))),
        check_vma=False,
    )
```

time: 82.7 us -> 76.6 us (0.926)
  local copies, waits for them, and re-layouts: 5.61 us -> 1.99 us
  Pallas kernels: 75.5 us -> 73.8 us
    unnamed x14 -> x4, local copies, waits for them, and re-layouts: 5.61 us -> 1.99 us
    pallas_call x1, Pallas kernels: 75.5 us -> 73.8 us  [body(): pl.pallas_call(functools.partial(kernel, n_z), out_shape=(jax.ShapeDtypeS...]
where the time goes in v2:
time: 76.6 us; the launch traced here: 76.4 us
  Pallas kernels  73.8 us (96%)
  local copies, waits for them, and re-layouts  1.99 us (3%)
    pallas_call x1, Pallas kernels, body(): pl.pallas_call(functools.partial(kernel, n_z), out_shape=(jax.ShapeDtypeS...  73.8 us
    unnamed x4, local copies, waits for them, and re-layouts  1.99 us

profile of v2, /device:TPU:1, one launch (start us, length us, event | category | flops | bytes accessed | tf_op | source)
XLA Modules:
  0.0 76.4 jit_solution(393743874633658191)
XLA Ops:
  0.6 73.8 %shard_map.77 = (bf16[64,512]{1,0:T(8,128)(2,1)}, f32[1,64]{1,0:T(1,128)}) custom-call(bf16[1024,512]{1,0:T(8,128)(2,1)} %src_hbm.1, bf16[1024,512]{1,0:T(8,128)(2,1)} %tgt_hbm.1, f32[8,128]{1,0:T(8,128)} %bitcast.4, f32[8,128]{1,0:T(8,128)} %bitcast.5, s32[1,1024]{1,0:T(1,128)} %bitcast.6, s32[1,12]{1,0:T(1,128)} %list_hbm.1), custom_call_target="tpu_custom_call" | custom-call | tf_op jit(solution)/shard_map/pallas_call | solution.py:388
  74.4 0.0 copy-start
  74.4 1.5 %copy.10 = bf16[64,512]{1,0:T(8,128)(2,1)} copy(bf16[64,512]{1,0:T(8,128)(2,1)} %get-tuple-element.8) | data formatting | bytes 131072
  75.9 0.0 copy-done
  75.9 0.5 copy.11
Async XLA Ops:
  74.4 1.5 %copy-start = (f32[1,64]{1,0:T(1,128)S(1)}, f32[1,64]{1,0:T(1,128)}, u32[]{:S(2)}) copy-start(f32[1,64]{1,0:T(1,128)} %get-tuple-element.5) | copy-start | bytes 772

commit v3 on v2

--- a/solution.py
+++ b/solution.py
@@ -428,15 +428,20 @@
             pltpu.SemaphoreType.DMA((21,)),
         ],
         compiler_params=pltpu.CompilerParams(
-            collective_id=0, has_side_effects=True, vmem_limit_bytes=64 * 1024 * 1024
+            collective_id=0, has_side_effects=True, vmem_limit_bytes=40 * 1024 * 1024
         ),
     )(
-        source_cells,
-        target_cells,
-        source_mass.reshape(8, 128),
-        target_mass.reshape(8, 128),
-        source_order.reshape(1, ROWS),
-        tile_list,
+        *[
+            pltpu.with_memory_space_constraint(operand, pltpu.HBM)
+            for operand in (
+                source_cells,
+                target_cells,
+                source_mass.reshape(8, 128),
+                target_mass.reshape(8, 128),
+                source_order.reshape(1, ROWS),
+                tile_list,
+            )
+        ]
     )
     return projected, log_mass.reshape(OUT)
 

time: 76.6 us -> 75.1 us (0.980)
  local copies, waits for them, and re-layouts: 1.99 us -> 1.14 us
    unnamed x4 -> x2, local copies, waits for them, and re-layouts: 1.99 us -> 1.14 us
where the time goes in v3:
time: 75.1 us; the launch traced here: 75 us
  Pallas kernels  73.2 us (97%)
  local copies, waits for them, and re-layouts  1.14 us (2%)
    pallas_call x1, Pallas kernels, body(): pl.pallas_call(functools.partial(kernel, n_z), out_shape=(jax.ShapeDtypeS...  73.2 us

profile of v3, /device:TPU:1, one launch (start us, length us, event | category | flops | bytes accessed | tf_op | source)
XLA Modules:
  0.0 75.0 jit_solution(5968665092542866212)
XLA Ops:
  0.6 73.2 %shard_map.77 = (bf16[64,512]{1,0:T(8,128)(2,1)S(1)}, f32[1,64]{1,0:T(1,128)S(1)}) custom-call(bf16[1024,512]{1,0:T(8,128)(2,1)} %src_hbm.1, bf16[1024,512]{1,0:T(8,128)(2,1)} %tgt_hbm.1, f32[8,128]{1,0:T(8,128)} %bitcast.5, f32[8,128]{1,0:T(8,128)} %bitcast.6, s32[1,1024]{1,0:T(1,128)} %bitcast.7, s32[1,12]{1,0:T(1,128)} %list_hbm.1), custom_call_target="tpu_custom_call" | custom-call | tf_op jit(solution)/shard_map/pallas_call | solution.py:388
  73.8 0.6 copy.10
  74.5 0.5 copy.11

commit v4 on v3

--- a/solution.py
+++ b/solution.py
@@ -18,8 +18,12 @@
 SHARPNESS = INVERSE_TEMP / EMB
 SLOTS = 12
 OUT = 64
-WIDE = EMB // 2
+PARTS = 4
+RELAYED = 2
+WIDE = EMB // PARTS
 FAR = 8
+COPIES = 9 * PARTS + 3 * RELAYED
+AHEAD = 2
 MESH = pl.DeviceIdType.MESH
 
 
@@ -241,15 +245,15 @@
         mine = col_product(src_scale)
         outbox[3 * i + 1] = mine
         broadcast(3 * i + 1, far_in.at[i], far_peers, 4 * i + 1)
-        broadcast(3 * i + 1, near_in.at[i], near_peers, 4 * i + 2)
+        broadcast(3 * i + 1, core_in.at[i], [sibling], 4 * i + 3)
+        arrived(core_in.at[i], 4 * i + 3)
+        mine = mine + core_in[i, 0]
+        outbox[3 * i + 2] = mine
+        broadcast(3 * i + 2, near_in.at[i], near_peers, 4 * i + 2)
         arrived(near_in.at[i], 4 * i + 2)
         mine = mine + jnp.sum(near_in[i], axis=0)
-        outbox[3 * i + 2] = mine
-        broadcast(3 * i + 2, core_in.at[i], [sibling], 4 * i + 3)
         arrived(far_in.at[i], 4 * i + 1)
-        mine = mine + jnp.sum(far_in[i], axis=0)
-        arrived(core_in.at[i], 4 * i + 3)
-        tgt_scale = power(tmass_ref[...] / (mine + core_in[i, 0]))
+        tgt_scale = power(tmass_ref[...] / (mine + jnp.sum(far_in[i], axis=0)))
 
     a = jnp.where(core == 0, x, y)
     b = jnp.where(core == 0, y, x)
@@ -267,12 +271,18 @@
             weighted = k_wide[pl.ds(chunk * OUT, OUT), :] * tgt_row
             scaled[e * OUT : (e + 1) * OUT, :] = weighted.astype(jnp.bfloat16)
 
-    def numerators(d, h):
-        num[h, d] = jnp.dot(
+    def numerators(d, first):
+        wide = jnp.dot(
             scaled[...],
-            tgt_ref[:, h * WIDE : (h + 1) * WIDE],
+            tgt_ref[:, first * WIDE : first * WIDE + BLK],
             preferred_element_type=jnp.float32,
-        ).reshape(4, OUT, WIDE)
+        )
+        for h in range(first, first + BLK // WIDE):
+            part = wide[:, (h - first) * WIDE : (h - first + 1) * WIDE]
+            num[h, d] = part.reshape(4, OUT, WIDE)
+        return range(first, first + BLK // WIDE)
+
+    firsts = range(0, PARTS, BLK // WIDE)
 
     started = []
 
@@ -294,20 +304,27 @@
     b_next, b_last, b_over = at(a, b + 1), at(a, b - 1), at(a, b + 2)
     first_p, first_m, direct, second = {}, {}, {}, {}
     scale_rows(2)
-    for h in range(2):
-        numerators(2, h)
-        first_p[h] = send(num.at[h, 2, 0:2], relay_p.at[h], a_next)
-        first_m[h] = send(num.at[h, 2, 2:4], relay_m.at[h], a_last)
+    for first in firsts:
+        for h in numerators(2, first):
+            first_p[h] = send(num.at[h, 2, 0:2], relay_p.at[h], a_next)
+            first_m[h] = send(num.at[h, 2, 2:4], relay_m.at[h], a_last)
     scale_rows(1)
-    for h in range(2):
-        numerators(1, h)
-        direct[h] = [send(num.at[h, 1, 2:4], from_m.at[h, 2:4], a_next)]
+    for first in firsts:
+        numerators(1, first)
     scale_rows(3)
-    for h in range(2):
-        numerators(3, h)
-        direct[h].append(send(num.at[h, 3, 0:2], from_p.at[h, 0:2], a_last))
-
-    for h in range(2):
+    for first in firsts:
+        numerators(3, first)
+    direct[0] = [
+        send(num.at[0, 1, 2:4], from_m.at[0, 2:4], a_next),
+        send(num.at[0, 3, 0:2], from_p.at[0, 0:2], a_last),
+    ]
+
+    for h in range(PARTS):
+        if h + 1 < PARTS:
+            direct[h + 1] = [
+                send(num.at[h + 1, 1, 2:4], from_m.at[h + 1, 2:4], a_next),
+                send(num.at[h + 1, 3, 0:2], from_p.at[h + 1, 0:2], a_last),
+            ]
         first_p[h].wait_recv()
         num[h, 1, 0:2] = num[h, 1, 0:2] + relay_p[h]
         second[h] = [send(num.at[h, 1, 0:2], from_m.at[h, 0:2], a_next)]
@@ -320,8 +337,8 @@
     broadcast(9, plane_in.at[3], plane_peers, 12)
 
     scale_rows(0)
-    for h in range(2):
-        numerators(0, h)
+    for first in firsts:
+        numerators(0, first)
 
     def gather(h):
         for copy in direct[h] + second[h]:
@@ -330,23 +347,32 @@
 
     half = OUT // 2
     up, down, over = (b + 1) % 4, (b + 3) % 4, (b + 2) % 4
-    gather(0)
-    far_p = send(num.at[0, 0, over, 0:half], relay2_p, b_next)
-    far_m = send(num.at[0, 0, over, half:OUT], relay2_m, b_last)
-    ends = [
-        send(num.at[0, 0, up, half:OUT], from2_m.at[0, half:OUT], b_next),
-        send(num.at[0, 0, down, 0:half], from2_p.at[0, 0:half], b_last),
-    ]
-    gather(1)
-    ends.append(send(num.at[1, 0, over], over2, b_over))
-    ends.append(send(num.at[1, 0, up], from2_m.at[1], b_next))
-    ends.append(send(num.at[1, 0, down], from2_p.at[1], b_last))
-    far_p.wait_recv()
-    num[0, 0, up, 0:half] = num[0, 0, up, 0:half] + relay2_p[...]
-    ends.append(send(num.at[0, 0, up, 0:half], from2_m.at[0, 0:half], b_next))
-    far_m.wait_recv()
-    num[0, 0, down, half:OUT] = num[0, 0, down, half:OUT] + relay2_m[...]
-    ends.append(send(num.at[0, 0, down, half:OUT], from2_p.at[0, half:OUT], b_last))
+    far_p, far_m = {}, {}
+    ends = {h: [] for h in range(PARTS)}
+
+    def pass_on(h):
+        far_p[h].wait_recv()
+        num[h, 0, up, 0:half] = num[h, 0, up, 0:half] + relay2_p[h]
+        ends[h].append(send(num.at[h, 0, up, 0:half], from2_m.at[h, 0:half], b_next))
+        far_m[h].wait_recv()
+        num[h, 0, down, half:OUT] = num[h, 0, down, half:OUT] + relay2_m[h]
+        ends[h].append(send(num.at[h, 0, down, half:OUT], from2_p.at[h, half:OUT], b_last))
+
+    for h in range(PARTS):
+        gather(h)
+        if h < RELAYED:
+            far_p[h] = send(num.at[h, 0, over, 0:half], relay2_p.at[h], b_next)
+            far_m[h] = send(num.at[h, 0, over, half:OUT], relay2_m.at[h], b_last)
+            ends[h].append(send(num.at[h, 0, up, half:OUT], from2_m.at[h, half:OUT], b_next))
+            ends[h].append(send(num.at[h, 0, down, 0:half], from2_p.at[h, 0:half], b_last))
+        else:
+            ends[h].append(send(num.at[h, 0, over], over2.at[h - RELAYED], b_over))
+            ends[h].append(send(num.at[h, 0, up], from2_m.at[h], b_next))
+            ends[h].append(send(num.at[h, 0, down], from2_p.at[h], b_last))
+        if h >= AHEAD and h - AHEAD < RELAYED:
+            pass_on(h - AHEAD)
+    for h in range(max(PARTS - AHEAD, 0), RELAYED):
+        pass_on(h)
 
     arrived(plane_in.at[3], 12)
     mass = mass + jnp.sum(plane_in[3], axis=0)
@@ -361,13 +387,6 @@
     lane_id = lax.broadcasted_iota(jnp.int32, (OUT, 128), 1)
     mass_col = jnp.sum(jnp.where(row_id == lane_id, mass_row, 0.0), axis=1, keepdims=True)
 
-    for copy in ends:
-        copy.wait_recv()
-    final = num[0, 0, b] + from2_m[0] + from2_p[0]
-    proj_ref[:, 0:WIDE] = (final / mass_col).astype(jnp.bfloat16)
-    final = num[1, 0, b] + from2_m[1] + from2_p[1] + over2[...]
-    proj_ref[:, WIDE:EMB] = (final / mass_col).astype(jnp.bfloat16)
-
     for i in range(ITERS):
         sent(plane_in.at[i], 4 * i)
         sent(far_in.at[i], 4 * i + 1)
@@ -376,6 +395,19 @@
     sent(plane_in.at[3], 12)
     for copy in started:
         copy.wait_send()
+
+    for h in range(PARTS):
+        for copy in ends[h]:
+            copy.wait_recv()
+        final = num[h, 0, b] + from2_m[h] + from2_p[h]
+        if h >= RELAYED:
+            final = final + over2[h - RELAYED]
+        proj_ref[:, h * WIDE : (h + 1) * WIDE] = (final / mass_col).astype(jnp.bfloat16)
+
+
+def hand_out(projected, log_mass, projected_out, log_out):
+    projected_out[...] = projected[...]
+    log_out[...] = log_mass[...]
 
 
 def body(n_z, source_cells, target_cells, source_mass, target_mass, source_order, tile_list, tile_count):
@@ -411,21 +443,21 @@
             pltpu.VMEM((3, far, 8, 128), f32),
             pltpu.VMEM((3, near, 8, 128), f32),
             pltpu.VMEM((3, 1, 8, 128), f32),
-            pltpu.VMEM((2, 4, 4, OUT, WIDE), f32),
-            pltpu.VMEM((2, 2, OUT, WIDE), f32),
-            pltpu.VMEM((2, 2, OUT, WIDE), f32),
-            pltpu.VMEM((2, 4, OUT, WIDE), f32),
-            pltpu.VMEM((2, 4, OUT, WIDE), f32),
-            pltpu.VMEM((half, WIDE), f32),
-            pltpu.VMEM((half, WIDE), f32),
-            pltpu.VMEM((2, OUT, WIDE), f32),
-            pltpu.VMEM((2, OUT, WIDE), f32),
-            pltpu.VMEM((OUT, WIDE), f32),
+            pltpu.VMEM((PARTS, 4, 4, OUT, WIDE), f32),
+            pltpu.VMEM((PARTS, 2, OUT, WIDE), f32),
+            pltpu.VMEM((PARTS, 2, OUT, WIDE), f32),
+            pltpu.VMEM((PARTS, 4, OUT, WIDE), f32),
+            pltpu.VMEM((PARTS, 4, OUT, WIDE), f32),
+            pltpu.VMEM((RELAYED, half, WIDE), f32),
+            pltpu.VMEM((RELAYED, half, WIDE), f32),
+            pltpu.VMEM((PARTS, OUT, WIDE), f32),
+            pltpu.VMEM((PARTS, OUT, WIDE), f32),
+            pltpu.VMEM((PARTS - RELAYED, OUT, WIDE), f32),
             pltpu.SemaphoreType.DMA((6,)),
             pltpu.SemaphoreType.DMA((13,)),
             pltpu.SemaphoreType.DMA((13,)),
-            pltpu.SemaphoreType.DMA((21,)),
-            pltpu.SemaphoreType.DMA((21,)),
+            pltpu.SemaphoreType.DMA((COPIES,)),
+            pltpu.SemaphoreType.DMA((COPIES,)),
         ],
         compiler_params=pltpu.CompilerParams(
             collective_id=0, has_side_effects=True, vmem_limit_bytes=40 * 1024 * 1024
@@ -443,6 +475,18 @@
             )
         ]
     )
+    projected, log_mass = pl.pallas_call(
+        hand_out,
+        out_shape=(
+            jax.ShapeDtypeStruct((OUT, EMB), bf16),
+            jax.ShapeDtypeStruct((1, OUT), f32),
+        ),
+        in_specs=[vmem] * 2,
+        out_specs=(vmem, vmem),
+    )(
+        pltpu.with_memory_space_constraint(projected, pltpu.VMEM),
+        pltpu.with_memory_space_constraint(log_mass, pltpu.VMEM),
+    )
     return projected, log_mass.reshape(OUT)
 
 

time: 75.1 us -> 74 us (0.985)
  local copies, waits for them, and re-layouts: 1.14 us -> 0 us
    unnamed x2 -> x0, local copies, waits for them, and re-layouts: 1.14 us -> none
where the time goes in v4:
time: 74 us; the launch traced here: 73.9 us
  Pallas kernels  73.3 us (99%)
    pallas_call x1, Pallas kernels, body(): pl.pallas_call(functools.partial(kernel, n_z), out_shape=(jax.ShapeDtypeS...  72.6 us

profile of v4, /device:TPU:1, one launch (start us, length us, event | category | flops | bytes accessed | tf_op | source)
XLA Modules:
  0.0 73.9 jit_solution(4229646572023106571)
XLA Ops:
  0.6 72.6 %shard_map.77 = (bf16[64,512]{1,0:T(8,128)(2,1)S(1)}, f32[1,64]{1,0:T(1,128)S(1)}) custom-call(bf16[1024,512]{1,0:T(8,128)(2,1)} %src_hbm.1, bf16[1024,512]{1,0:T(8,128)(2,1)} %tgt_hbm.1, f32[8,128]{1,0:T(8,128)} %bitcast.4, f32[8,128]{1,0:T(8,128)} %bitcast.5, s32[1,1024]{1,0:T(1,128)} %bitcast.6, s32[1,12]{1,0:T(1,128)} %list_hbm.1), custom_call_target="tpu_custom_call" | custom-call | tf_op jit(solution)/shard_map/pallas_call | solution.py:420
  73.3 0.6 shard_map.78

commit v5 on v4

--- a/solution.py
+++ b/solution.py
@@ -35,7 +35,7 @@
         hat[rows, :] = (wide * lax.rsqrt(mean + NORM_EPSILON)).astype(jnp.bfloat16)
         return carry
 
-    lax.fori_loop(0, ROWS // BLK, step, 0)
+    lax.fori_loop(0, ROWS // BLK, step, 0, unroll=True)
 
 
 def power(x):
@@ -84,6 +84,7 @@
     list_ref,
     src_hat,
     tgt_hat,
+    links,
     k_wide,
     k_half,
     k_turned,
@@ -103,6 +104,7 @@
     from2_m,
     from2_p,
     over2,
+    passed_on,
     load_sem,
     small_send,
     small_recv,
@@ -131,32 +133,31 @@
     def device(where):
         return {"src": where[0], "tgt": where[1]}
 
+    loads = {}
+
+    def load(name, there, here):
+        loads[name] = pltpu.make_async_copy(there, here, load_sem.at[len(loads)])
+        loads[name].start()
+
+    load("order", order_hbm, order_ref)
+    load("list", list_hbm, list_ref)
+    for i in range(ROWS // BLK):
+        rows = pl.ds(i * BLK, BLK)
+        load(("tgt", i), tgt_hbm.at[rows], tgt_ref.at[rows])
+        load(("src", i), src_hbm.at[rows], src_ref.at[rows])
+    load("smass", smass_hbm, smass_ref)
+    load("tmass", tmass_hbm, tmass_ref)
+
     barrier = pltpu.get_barrier_semaphore()
-    everyone = far_peers + near_peers + plane_peers + [sibling]
-    for where in everyone:
+    reach = n_z // 4
+    relays = [((z + d) % n_z * 2 + core, t) for d in (reach, n_z - reach)]
+    greeted = [((z + d) % n_z * 2 + 1 - core, t) for d in (reach, n_z - reach)]
+    greeted += [((z + d) % n_z * 2 + core, t) for d in z_steps if min(d, n_z - d) <= reach]
+    greeted += plane_peers + [sibling]
+    for where in greeted:
         pl.semaphore_signal(barrier, 1, device_id=device(where), device_id_type=MESH)
-    loads = [
-        pltpu.make_async_copy(there, here, load_sem.at[i])
-        for i, (there, here) in enumerate(
-            (
-                (src_hbm, src_ref),
-                (tgt_hbm, tgt_ref),
-                (order_hbm, order_ref),
-                (list_hbm, list_ref),
-                (smass_hbm, smass_ref),
-                (tmass_hbm, tmass_ref),
-            )
-        )
-    ]
-    for load in loads:
-        load.start()
-    loads[0].wait()
-    normalize_into(src_ref, src_hat)
-    loads[1].wait()
-    normalize_into(tgt_ref, tgt_hat)
-    for load in loads[2:]:
-        load.wait()
-
+    loads["order"].wait()
+    loads["list"].wait()
     codes = jnp.maximum(list_ref[...], 0)
     live = list_ref[...] >= 0
     flags = jnp.where(live, jnp.int32(1) << codes, 0).astype(jnp.float32)
@@ -165,11 +166,26 @@
     bits_row = jnp.broadcast_to(bits, (1, ROWS))
     nibble = (lax.shift_right_logical(bits_row, (position // BLK) * 4) & 15).astype(jnp.float32)
 
+    def find_links(i, carry):
+        row_ids = lax.broadcasted_iota(jnp.int32, (BLK, 1), 0) + i * BLK
+        placed = jnp.where(order_ref[...] == row_ids, nibble, 0.0)
+        links[pl.ds(i * BLK, BLK), :] = jnp.sum(placed, axis=1, keepdims=True)
+        return carry
+
+    lax.fori_loop(0, ROWS // BLK, find_links, 0, unroll=True)
+
+    for i in range(ROWS // BLK):
+        loads["tgt", i].wait()
+    normalize_into(tgt_ref, tgt_hat)
+    for i in range(ROWS // BLK):
+        loads["src", i].wait()
+    normalize_into(src_ref, src_hat)
+    loads["smass"].wait()
+    loads["tmass"].wait()
+
     def build(i, carry):
         rows = pl.ds(i * BLK, BLK)
-        row_ids = lax.broadcasted_iota(jnp.int32, (BLK, 1), 0) + i * BLK
-        placed = jnp.where(order_ref[...] == row_ids, nibble, 0.0)
-        links = jnp.sum(placed, axis=1, keepdims=True).astype(jnp.int32)
+        linked_to = links[rows, :].astype(jnp.int32)
         for q in range(COLS // BLK):
             cols = pl.ds(q * BLK, BLK)
             similarity = lax.dot_general(
@@ -178,13 +194,13 @@
                 (((1,), (1,)), ((), ())),
                 preferred_element_type=jnp.float32,
             )
-            linked = (lax.shift_right_logical(links, q) & 1).astype(jnp.float32)
+            linked = (lax.shift_right_logical(linked_to, q) & 1).astype(jnp.float32)
             tile = jnp.exp(similarity * SHARPNESS) * linked
             k_wide[rows, cols] = tile
             k_half[rows, cols] = tile.astype(jnp.bfloat16)
         return carry
 
-    lax.fori_loop(0, ROWS // BLK, build, 0)
+    lax.fori_loop(0, ROWS // BLK, build, 0, unroll=True)
 
     def turn(i, carry):
         rows = pl.ds(i * BLK, BLK)
@@ -232,7 +248,9 @@
 
     tgt_scale = jnp.ones((8, 128), jnp.float32)
     src_scale = jnp.ones((8, 128), jnp.float32)
-    pl.semaphore_wait(barrier, len(everyone))
+    pl.semaphore_wait(barrier, len(greeted))
+    for where in relays:
+        pl.semaphore_signal(passed_on, 1, device_id=device(where), device_id_type=MESH)
     for i in range(ITERS):
         mine = row_product(tgt_scale) if i else first_row_product(tgt_scale)
         outbox[3 * i] = mine
@@ -244,6 +262,8 @@
 
         mine = col_product(src_scale)
         outbox[3 * i + 1] = mine
+        if i == 0:
+            pl.semaphore_wait(passed_on, len(relays))
         broadcast(3 * i + 1, far_in.at[i], far_peers, 4 * i + 1)
         broadcast(3 * i + 1, core_in.at[i], [sibling], 4 * i + 3)
         arrived(core_in.at[i], 4 * i + 3)
@@ -434,6 +454,7 @@
             pltpu.VMEM((1, SLOTS), i32),
             pltpu.VMEM((ROWS, EMB), bf16),
             pltpu.VMEM((COLS, EMB), bf16),
+            pltpu.VMEM((ROWS, 1), f32),
             pltpu.VMEM((ROWS, COLS), f32),
             pltpu.VMEM((ROWS, COLS), bf16),
             pltpu.VMEM((COLS, ROWS), bf16),
@@ -453,7 +474,8 @@
             pltpu.VMEM((PARTS, OUT, WIDE), f32),
             pltpu.VMEM((PARTS, OUT, WIDE), f32),
             pltpu.VMEM((PARTS - RELAYED, OUT, WIDE), f32),
-            pltpu.SemaphoreType.DMA((6,)),
+            pltpu.SemaphoreType.REGULAR,
+            pltpu.SemaphoreType.DMA((12,)),
             pltpu.SemaphoreType.DMA((13,)),
             pltpu.SemaphoreType.DMA((13,)),
             pltpu.SemaphoreType.DMA((COPIES,)),

time: 74 us -> 71.6 us (0.968)
  Pallas kernels: 73.3 us -> 70.6 us
    pallas_call x1, Pallas kernels: 72.6 us -> 69.9 us  [body(): pl.pallas_call(functools.partial(kernel, n_z), out_shape=(jax.ShapeDtypeS...]
where the time goes in v5:
time: 71.6 us; the launch traced here: 71.2 us
  Pallas kernels  70.6 us (99%)
    pallas_call x1, Pallas kernels, body(): pl.pallas_call(functools.partial(kernel, n_z), out_shape=(jax.ShapeDtypeS...  69.9 us

profile of v5, /device:TPU:1, one launch (start us, length us, event | category | flops | bytes accessed | tf_op | source)
XLA Modules:
  0.0 71.2 jit_solution(17719641126865913530)
XLA Ops:
  0.6 69.9 %shard_map.77 = (bf16[64,512]{1,0:T(8,128)(2,1)S(1)}, f32[1,64]{1,0:T(1,128)S(1)}) custom-call(bf16[1024,512]{1,0:T(8,128)(2,1)} %src_hbm.1, bf16[1024,512]{1,0:T(8,128)(2,1)} %tgt_hbm.1, f32[8,128]{1,0:T(8,128)} %bitcast.4, f32[8,128]{1,0:T(8,128)} %bitcast.5, s32[1,1024]{1,0:T(1,128)} %bitcast.6, s32[1,12]{1,0:T(1,128)} %list_hbm.1), custom_call_target="tpu_custom_call" | custom-call | tf_op jit(solution)/shard_map/pallas_call | solution.py:440
  70.6 0.6 shard_map.78
